TPU v7x, 256 devices: a whole 4x4x8 slice. The times are simulated.
256 devices in a mesh: group: 4 (over y), dev: 64 (over z, x, core).
Axes of the slice: x: 4, y: 4, z: 8, core: 2. Of those that a mesh axis runs over, the one named last changes fastest.
Arguments:
- history: bfloat16 [256, 48, 64, 256], P(('group', 'dev')), may hold values from -6 to 6
- incident: float32 [256, 3, 64, 256], P(('group', 'dev')), may hold values from -6 to 6
- jacobi: float32 [256, 256, 256], P(('group', 'dev')), may hold values from -0.375 to 0.375
- self_tiles: bfloat16 [256, 2, 256, 256], P(('group', 'dev')), may hold values from -0.25 to 0.25
- near_tiles: bfloat16 [256, 76, 256, 256], P(('group', 'dev')), may hold values from -0.0390625 to 0.0390625
- send_lag: int32 [256, 64, 1], P(('group', 'dev')), may hold values from 3 to 48
- cross_lag: int32 [256, 4, 2], P(('group', 'dev')), may hold values from 3 to 48
- tile_slot: int32 [256, 76], P(('group', 'dev')), may hold values from 0 to 71, as said below
- tile_dest: int32 [256, 76], P(('group', 'dev')), may hold values from 0 to 63
Outputs:
- solution: float32 [256, 3, 64, 256], P(('group', 'dev'))
Inputs may be any that keep to these rules, and one draw needn't show every extreme that they name: `tile_slot`: every slot index 0 .. 71 is read by at least one tile of every device; the other tiles read any slot.
All inputs are finite; a program needn't handle non-finite values.
Results may differ from a plain program's by a relative error of at most 0.0022.
Values may be sent and summed in bfloat16 or wider, within the bound.
A program may use at most 128 MiB of HBM per device.

v0:
```python
import jax
import jax.numpy as jnp
from jax import lax
from jax.sharding import PartitionSpec as P

STEPS = 3


def prepare_terms(received, near_tiles, tile_slot, tile_dest, ndev):
    tiles = near_tiles[0]
    values = received[:, tile_slot[0]]
    product = jnp.einsum("strp,tpq->tsrq", values, tiles, preferred_element_type=jnp.float32)
    flat = product.reshape(product.shape[0], -1)
    grouped = jax.ops.segment_sum(flat, tile_dest[0], num_segments=ndev)

    def partial_rows(start, count):
        return grouped

    return partial_rows


def per_device(
    history, incident, jacobi, self_tiles, near_tiles, send_lag, cross_lag, tile_slot, tile_dest
):
    ndev = lax.axis_size("dev")
    own = history[0]
    width = own.shape[1]
    panels = own.shape[2]
    remote = []
    for step in range(STEPS):
        blocks = own[send_lag[0] - step - 1]
        inner = lax.all_to_all(blocks, "dev", split_axis=0, concat_axis=0, tiled=True).reshape(
            -1, width, panels
        )
        crossing = own[cross_lag[0] - step - 1]
        outer = lax.all_to_all(crossing, "group", split_axis=0, concat_axis=0, tiled=True).reshape(
            -1, width, panels
        )
        received = jnp.concatenate([inner, outer], axis=0)[None]
        partial_rows = prepare_terms(received, near_tiles, tile_slot, tile_dest, ndev)
        summed = lax.psum_scatter(
            partial_rows(jnp.int32(0), 1 * lax.axis_size("dev")),
            "dev",
            scatter_dimension=0,
            tiled=True,
        )
        remote.append(summed.reshape(width, panels))
    first_tile = self_tiles[0, 0]
    second_tile = self_tiles[0, 1]
    inverse = jacobi[0]
    prior_one = own[0]
    prior_two = own[1]
    solved = []
    for step in range(STEPS):
        selfterm = jnp.dot(prior_one, first_tile, preferred_element_type=jnp.float32)
        selfterm = selfterm + jnp.dot(prior_two, second_tile, preferred_element_type=jnp.float32)
        resid = incident[0, step] - remote[step] - selfterm
        value = jnp.dot(
            resid, inverse, precision=lax.Precision.HIGHEST, preferred_element_type=jnp.float32
        )
        solved.append(value)
        prior_two = prior_one
        prior_one = value.astype(jnp.bfloat16)
    return jnp.stack(solved, axis=0)[None]


def solution(mesh):
    return jax.shard_map(
        per_device,
        mesh=mesh,
        in_specs=(
            P(("group", "dev"), None, None, None),
            P(("group", "dev"), None, None, None),
            P(("group", "dev"), None, None),
            P(("group", "dev"), None, None, None),
            P(("group", "dev"), None, None, None),
            P(("group", "dev"), None, None),
            P(("group", "dev"), None, None),
            P(("group", "dev"), None),
            P(("group", "dev"), None),
        ),
        out_specs=P(("group", "dev"), None, None, None),
        check_vma=False,
    )
```

profile of v0, /device:TPU:8, one launch (start us, length us, event | category | flops | bytes accessed | tf_op | source)
XLA Modules:
  0.0 487.4 jit_solution(2052571655852376418)
XLA Ops:
  6.5 0.8 compare_select_fusion
  7.6 2.7 gather_fusion.1
  10.2 5.6 %all-to-all-start.1 = ((bf16[4,2,64,256]{3,2,1,0:T(8,128)(2,1)}), bf16[4,2,64,256]{3,2,1,0:T(8,128)(2,1)S(1)}, u32[]{:S(2)}, u32[]{:S(2)}) async-start(bf16[4,2,64,256]{3,2,1,0:T(8,128)(2,1)} %bitcast.10), calls=%async_computation.1 | async-start | bytes 524288 | tf_op jit(solution)/shard_map/all_to_all | solution.py:36
  16.0 2.7 gather_fusion.4
  18.6 2.4 all-to-all-done.1
  21.0 4.8 all-to-all-start.3
  26.0 2.7 gather_fusion.7
  28.7 2.4 all-to-all-done.3
  31.1 4.8 all-to-all-start.5
  35.9 2.0 gather_fusion
  38.0 3.2 all-to-all-done.5
  41.1 11.6 %all-to-all-start = ((bf16[64,1,64,256]{3,2,1,0:T(8,128)(2,1)}), bf16[64,1,64,256]{3,2,1,0:T(8,128)(2,1)}, u32[]{:S(2)}, u32[]{:S(2)}) async-start(bf16[64,1,64,256]{3,2,1,0:T(8,128)(2,1)} %bitcast.135), calls=%async_computation | async-start | bytes 4194304 | tf_op jit(solution)/shard_map/all_to_all | solution.py:32
  52.7 2.0 gather_fusion.3
  54.7 49.1 %all-to-all-done = bf16[64,1,64,256]{3,2,1,0:T(8,128)(2,1)} async-done(((bf16[64,1,64,256]{3,2,1,0:T(8,128)(2,1)}), bf16[64,1,64,256]{3,2,1,0:T(8,128)(2,1)}, u32[]{:S(2)}, u32[]{:S(2)}) %all-to-all-start) | async-done | bytes 2097184 | tf_op jit(solution)/shard_map/all_to_all | solution.py:32
  103.9 5.6 %all-to-all-start.2 = ((bf16[64,1,64,256]{3,2,1,0:T(8,128)(2,1)}), bf16[64,1,64,256]{3,2,1,0:T(8,128)(2,1)}, u32[]{:S(2)}, u32[]{:S(2)}) async-start(bf16[64,1,64,256]{3,2,1,0:T(8,128)(2,1)} %bitcast.134), calls=%async_computation.2 | async-start | bytes 4194304 | tf_op jit(solution)/shard_map/all_to_all | solution.py:32
  109.5 2.0 gather_fusion.6
  111.5 49.2 %all-to-all-done.2 = bf16[64,1,64,256]{3,2,1,0:T(8,128)(2,1)} async-done(((bf16[64,1,64,256]{3,2,1,0:T(8,128)(2,1)}), bf16[64,1,64,256]{3,2,1,0:T(8,128)(2,1)}, u32[]{:S(2)}, u32[]{:S(2)}) %all-to-all-start.2) | async-done | bytes 2097184 | tf_op jit(solution)/shard_map/all_to_all | solution.py:32
  160.7 5.6 %all-to-all-start.4 = ((bf16[64,1,64,256]{3,2,1,0:T(8,128)(2,1)}), bf16[64,1,64,256]{3,2,1,0:T(8,128)(2,1)}, u32[]{:S(2)}, u32[]{:S(2)}) async-start(bf16[64,1,64,256]{3,2,1,0:T(8,128)(2,1)} %bitcast.133), calls=%async_computation.4 | async-start | bytes 4194304 | tf_op jit(solution)/shard_map/all_to_all | solution.py:32
  166.3 0.5 all-reduce.6.cloned.1.call-start
  166.8 3.3 pad_maximum_fusion
  170.1 4.1 gather_fusion.2
  174.2 6.4 %fusion.4 = f32[76,64,256]{2,1,0:T(8,128)S(1)} fusion(bf16[76,64,256]{2,1,0:T(8,128)(2,1)} %gather_fusion.2, bf16[1,76,256,256]{3,2,1,0:T(8,128)(2,1)} %param.13), kind=kOutput, calls=%fused_computation.16 | convolution fusion | flops 637534208 | bytes 17432576 | tf_op jit(solution)/shard_map/strp,tpq->tsrq/dot_general | solution.py:12
  180.6 0.8 pad.18
  181.4 5.6 %copy.19 = f32[10,8,64,256]{3,1,2,0:T(8,128)} copy(f32[10,8,64,256]{3,2,1,0:T(8,128)S(1)} %bitcast.130) | data formatting | bytes 10485760
  187.1 3.2 pad_maximum_fusion.1
  190.3 4.0 gather_fusion.5
  194.3 6.4 %fusion.2 = f32[76,64,256]{2,1,0:T(8,128)S(1)} fusion(bf16[76,64,256]{2,1,0:T(8,128)(2,1)} %gather_fusion.5, bf16[1,76,256,256]{3,2,1,0:T(8,128)(2,1)} %param.13), kind=kOutput, calls=%fused_computation.14 | convolution fusion | flops 637534208 | bytes 17432576 | tf_op jit(solution)/shard_map/strp,tpq->tsrq/dot_general | solution.py:12
  200.7 0.8 pad.19
  201.5 5.6 %copy.20 = f32[10,8,64,256]{3,1,2,0:T(8,128)} copy(f32[10,8,64,256]{3,2,1,0:T(8,128)S(1)} %bitcast.131) | data formatting | bytes 10485760
  207.1 10.3 %scatter_custom_fusion = f32[64,16384]{1,0:T(8,128)} fusion(s32[76]{0:T(128)} %bitcast.144, f32[76,16384]{1,0:T(8,128)} %bitcast.136, f32[]{:T(128)} %constant.29.clone.1), kind=kCustom, calls=%fused_computation.25 | custom fusion | flops 1245184 | bytes 4194816 | tf_op jit(solution)/shard_map/scatter-add | solution.py:14
  217.4 10.3 %scatter_custom_fusion.1 = f32[64,16384]{1,0:T(8,128)} fusion(s32[76]{0:T(128)} %bitcast.145, f32[76,16384]{1,0:T(8,128)} %bitcast.137, f32[]{:T(128)} %constant.29.clone.1), kind=kCustom, calls=%fused_computation.23 | custom fusion | flops 1245184 | bytes 4194816 | tf_op jit(solution)/shard_map/scatter-add | solution.py:14
  227.7 3.2 pad_maximum_fusion.2
  231.0 4.0 gather_fusion.8
  235.0 6.4 %fusion = f32[76,64,256]{2,1,0:T(8,128)S(1)} fusion(bf16[76,64,256]{2,1,0:T(8,128)(2,1)} %gather_fusion.8, bf16[1,76,256,256]{3,2,1,0:T(8,128)(2,1)} %param.13), kind=kOutput, calls=%fused_computation.12 | convolution fusion | flops 637534208 | bytes 17432576 | tf_op jit(solution)/shard_map/strp,tpq->tsrq/dot_general | solution.py:12
  241.4 0.8 pad.20
  242.2 5.5 %copy.21 = f32[10,8,64,256]{3,1,2,0:T(8,128)} copy(f32[10,8,64,256]{3,2,1,0:T(8,128)S(1)} %bitcast.132) | data formatting | bytes 10485760
  247.8 10.1 %scatter_custom_fusion.2 = f32[64,16384]{1,0:T(8,128)} fusion(s32[76]{0:T(128)} %bitcast.146, f32[76,16384]{1,0:T(8,128)} %bitcast.138, f32[]{:T(128)} %constant.29.clone.1), kind=kCustom, calls=%fused_computation.21 | custom fusion | flops 1245184 | bytes 4194816 | tf_op jit(solution)/shard_map/scatter-add | solution.py:14
  257.9 0.6 copy-done.6
  258.6 0.6 dynamic-slice
  259.3 214.7 %all-reduce.6.cloned.1.call-done = (f32[64,16384]{1,0:T(8,128)}, f32[64,16384]{1,0:T(8,128)}, f32[64,16384]{1,0:T(8,128)}) async-done(((f32[64,16384]{1,0:T(8,128)}, f32[64,16384]{1,0:T(8,128)}, f32[64,16384]{1,0:T(8,128)}), (f32[64,16384]{1,0:T(8,128)}, f32[64,16384]{1,0:T(8,128)}, f32[64,16384]{1,0:T(8,128)})) %all-reduce.6.cloned.1.call-update) | async-done | bytes 12582928
  473.9 2.2 dynamic-slice_reduce_fusion
  476.2 1.9 dynamic-slice_reduce_fusion.2
  478.1 0.1 fusion.14
  478.2 0.2 fusion.18
  478.6 0.2 fusion.13
  478.8 0.3 fusion.16
  479.4 0.3 convolution_bitcast_fusion
  479.7 0.7 maximum_bitcast_fusion
  (37 shorter events, 1.3 us)
Async XLA Ops:
  6.5 471.7 %copy-start = (f32[1,256,256]{2,1,0:T(8,128)S(1)}, f32[1,256,256]{2,1,0:T(8,128)}, u32[]{:S(2)}) copy-start(f32[1,256,256]{2,1,0:T(8,128)} %param.11) | copy-start | bytes 786436
  6.5 29.4 %copy-start.1 = (bf16[1,48,64,256]{3,2,1,0:T(8,128)(2,1)S(1)}, bf16[1,48,64,256]{3,2,1,0:T(8,128)(2,1)}, u32[]{:S(2)}) copy-start(bf16[1,48,64,256]{3,2,1,0:T(8,128)(2,1)} %param.9) | copy-start | bytes 4718596
  6.5 29.4 %copy-start.4 = (s32[1,64,1]{1,2,0:T(1,128)S(1)}, s32[1,64,1]{1,2,0:T(1,128)}, u32[]{:S(2)}) copy-start(s32[1,64,1]{1,2,0:T(1,128)} %param.14) | copy-start | bytes 772
  10.2 10.8 %all-to-all-start.1 = ((bf16[4,2,64,256]{3,2,1,0:T(8,128)(2,1)}), bf16[4,2,64,256]{3,2,1,0:T(8,128)(2,1)S(1)}, u32[]{:S(2)}, u32[]{:S(2)}) async-start(bf16[4,2,64,256]{3,2,1,0:T(8,128)(2,1)} %bitcast.10), calls=%async_computation.1 | async-start | bytes 524288 | tf_op jit(solution)/shard_map/all_to_all | solution.py:36
  21.0 10.1 %all-to-all-start.3 = ((bf16[4,2,64,256]{3,2,1,0:T(8,128)(2,1)}), bf16[4,2,64,256]{3,2,1,0:T(8,128)(2,1)S(1)}, u32[]{:S(2)}, u32[]{:S(2)}) async-start(bf16[4,2,64,256]{3,2,1,0:T(8,128)(2,1)} %bitcast.29), calls=%async_computation.3 | async-start | bytes 524288 | tf_op jit(solution)/shard_map/all_to_all | solution.py:36
  31.1 10.1 %all-to-all-start.5 = ((bf16[4,2,64,256]{3,2,1,0:T(8,128)(2,1)}), bf16[4,2,64,256]{3,2,1,0:T(8,128)(2,1)S(1)}, u32[]{:S(2)}, u32[]{:S(2)}) async-start(bf16[4,2,64,256]{3,2,1,0:T(8,128)(2,1)} %bitcast.40), calls=%async_computation.5 | async-start | bytes 524288 | tf_op jit(solution)/shard_map/all_to_all | solution.py:36
  41.1 62.8 %all-to-all-start = ((bf16[64,1,64,256]{3,2,1,0:T(8,128)(2,1)}), bf16[64,1,64,256]{3,2,1,0:T(8,128)(2,1)}, u32[]{:S(2)}, u32[]{:S(2)}) async-start(bf16[64,1,64,256]{3,2,1,0:T(8,128)(2,1)} %bitcast.135), calls=%async_computation | async-start | bytes 4194304 | tf_op jit(solution)/shard_map/all_to_all | solution.py:32
  103.9 56.8 %all-to-all-start.2 = ((bf16[64,1,64,256]{3,2,1,0:T(8,128)(2,1)}), bf16[64,1,64,256]{3,2,1,0:T(8,128)(2,1)}, u32[]{:S(2)}, u32[]{:S(2)}) async-start(bf16[64,1,64,256]{3,2,1,0:T(8,128)(2,1)} %bitcast.134), calls=%async_computation.2 | async-start | bytes 4194304 | tf_op jit(solution)/shard_map/all_to_all | solution.py:32
  111.5 55.3 %copy-start.5 = (s32[1,76]{1,0:T(1,128)S(1)}, s32[1,76]{1,0:T(1,128)}, u32[]{:S(2)}) copy-start(s32[1,76]{1,0:T(1,128)} %param.16) | copy-start | bytes 916
  160.7 67.0 %all-to-all-start.4 = ((bf16[64,1,64,256]{3,2,1,0:T(8,128)(2,1)}), bf16[64,1,64,256]{3,2,1,0:T(8,128)(2,1)}, u32[]{:S(2)}, u32[]{:S(2)}) async-start(bf16[64,1,64,256]{3,2,1,0:T(8,128)(2,1)} %bitcast.133), calls=%async_computation.4 | async-start | bytes 4194304 | tf_op jit(solution)/shard_map/all_to_all | solution.py:32
  166.3 307.6 %all-reduce.6.cloned.1.call-start = ((), (), s32[]{:S(2)}) async-start(), calls=%async_computation.6 | async-start | bytes 25165824
  257.9 0.7 copy-start.6
  257.9 1.3 copy-start.2
  257.9 220.2 %copy-start.3 = (f32[1,3,64,256]{3,2,1,0:T(8,128)S(1)}, f32[1,3,64,256]{3,2,1,0:T(8,128)}, u32[]{:S(2)}) copy-start(f32[1,3,64,256]{3,2,1,0:T(8,128)} %param.10) | copy-start | bytes 589828
Sparse Core Ops, SparseCore 0:
  258.0 215.8 all-reduce.5
where the time goes:
time: 492 us; the launch traced here: 487 us
  waiting for transfers between devices  321 us (65%)
  local copies, waits for them, and re-layouts  51.3 us (10%)
  other arithmetic  42 us (9%)
  starting transfers between devices  38.5 us (8%)
  matrix products  20.9 us (4%)
  between operations  13.9 us (3%)
    unnamed x2, waiting for transfers between devices  215 us
    all_to_all x3, waiting for transfers between devices, per_device(): lax.all_to_all(blocks, 'dev', split_axis=0, concat_axis=0, tiled=True)  98.3 us
    scatter-add x3, other arithmetic, prepare_terms(): grouped = jax.ops.segment_sum(flat, tile_dest[0], num_segments=ndev)  30.7 us
    unnamed x23, local copies, waits for them, and re-layouts  24.5 us
    all_to_all x3, starting transfers between devices, per_device(): lax.all_to_all(blocks, 'dev', split_axis=0, concat_axis=0, tiled=True)  22.7 us
    dot_general x3, matrix products, prepare_terms(): jnp.einsum('strp,tpq->tsrq', values, tiles, preferred_element_type=jnp.fl...  19.3 us
    all_to_all x3, starting transfers between devices, per_device(): lax.all_to_all(crossing, 'group', split_axis=0, concat_axis=0, tiled=True)  15.2 us
    gather x3, local copies, waits for them, and re-layouts, prepare_terms(): values = received[:, tile_slot[0]]  12.1 us
  transfers between devices with their start and end apart: 7, of which 6 were waited for; matrix products, arithmetic and copies ran while one was open for 15% of the time, Pallas kernels for 0%

commit v1 on v0

v1 whole, which is shorter than its diff:
```python
import functools

import jax
import jax.numpy as jnp
from jax import lax
from jax.experimental import pallas as pl
from jax.experimental.pallas import tpu as pltpu
from jax.sharding import PartitionSpec as P

MESH = pl.DeviceIdType.MESH
Z, X, C = 8, 4, 2
S = X * C
G = 4
LAGS, R, W, STEPS = 48, 64, 256, 3
TILES = 76
SLOTS = Z * S + 2 * G
CH = 4
RC = R // CH
ROWS = STEPS * RC
F32, BF16, I32 = jnp.float32, jnp.bfloat16, jnp.int32
SEND1, SEND2, SEND3 = F32, BF16, BF16
UNROLL = 4


def kernel(
    meta, hist, inc_hbm, jac_hbm, self_hbm, tiles_hbm, out,
    hists, pkt3, pkt4, fsel, sel, csel, recvs, tiles, inc, jac, selft,
    cum, send1, r1, send2, own2, r2, send3, own3, r3,
    lagbuf, srt, slag, ssrt,
    load_sem, in_sem, lag_s, lag_r, small_sem,
    h_s, h_r, x_s, x_r, rs_s, rs_r,
):
    dev, g = lax.axis_index("dev"), lax.axis_index("group")
    z, x, c = dev // S, (dev // C) % X, dev % C
    me = x * C + c

    def at(zz, xx, cc):
        return (g, (zz * X + xx) * C + cc)

    def zpeer(dz):
        return at(lax.rem(z + dz + Z, Z), x, c)

    def plane(n):
        return (g, z * S + n)

    def remote(src, dst, ss, rs, dev_id):
        cp = pltpu.make_async_remote_copy(
            src_ref=src, dst_ref=dst, send_sem=ss, recv_sem=rs, device_id=dev_id, device_id_type=MESH
        )
        cp.start()
        return cp

    loads = []
    for j in range(CH):
        cp = pltpu.make_async_copy(hist.at[:, pl.ds(j * RC, RC), :], hists[0][j], load_sem.at[j])
        cp.start()
        loads.append(cp)
    big = [
        pltpu.make_async_copy(tiles_hbm, tiles, in_sem.at[0]),
        pltpu.make_async_copy(inc_hbm, inc, in_sem.at[1]),
        pltpu.make_async_copy(jac_hbm, jac, in_sem.at[2]),
        pltpu.make_async_copy(self_hbm, selft, in_sem.at[3]),
    ]

    barrier = pltpu.get_barrier_semaphore()
    for dz in range(1, Z):
        pl.semaphore_signal(barrier, inc=1, device_id=zpeer(dz), device_id_type=MESH)
    for i in range(1, S):
        pl.semaphore_signal(barrier, inc=1, device_id=plane(lax.rem(me + i, S)), device_id_type=MESH)
    for i in range(1, G):
        pl.semaphore_signal(barrier, inc=1, device_id=(lax.rem(g + i, G), dev), device_id_type=MESH)
    pl.semaphore_wait(barrier, Z - 1 + S - 1 + G - 1)

    sent = []
    hops = {}

    def h1(j):
        loads[j].wait()
        for d, dz in ((0, 1), (1, -1)):
            hops[1, j, d] = remote(hists[0][j], hists[1 + d][j], h_s.at[0, j, d], h_r.at[0, j, d], zpeer(dz))

    def h2(j):
        for d, dz in ((0, 1), (1, -1)):
            hops[1, j, d].wait_recv()
            hops[2, j, d] = remote(hists[1 + d][j], hists[3 + d][j], h_s.at[1, j, d], h_r.at[1, j, d], zpeer(dz))

    def h3(j):
        for d, dz in ((0, 1), (1, -1)):
            hops[2, j, d].wait_recv()
            near = lax.rem(z + dz + Z, Z) * S
            far = lax.rem(z + 2 * dz + Z, Z) * S + d * (S // 2)

            @pl.loop(0, S)
            def _(n):
                fsel[d, j, n] = hists[3 + d][j][pl.ds(slag[3 + d, 0, near + n], STEPS)]

            @pl.loop(0, S // 2)
            def _(n):
                fsel[d, j, S + n] = hists[3 + d][j][pl.ds(slag[3 + d, 0, far + n], STEPS)]

            hops[3, j, d] = remote(fsel.at[d, j], pkt3.at[d, j], h_s.at[2, j, d], h_r.at[2, j, d], zpeer(dz))

    def xsend(j, pick, width, col):
        for i in range(1, S):
            n = lax.rem(me + i, S)
            remote(pick(n), recvs[j].at[pl.ds(me * Z + col, width)], x_s.at[j], x_r.at[j], plane(n))
        pltpu.make_async_copy(pick(me), recvs[j].at[pl.ds(me * Z + col, width)], x_r.at[j]).start()

    def xa(j):
        for o in range(5):

            @pl.loop(0, S)
            def _(n):
                sel[j, n, o] = hists[o][j][pl.ds(slag[o, 0, z * S + n], STEPS)]

        xsend(j, lambda n: sel.at[j, n], 5, 0)

    def h4(j):
        for d, dz in ((0, 1), (1, -1)):
            hops[3, j, d].wait_recv()
            hops[4, j, d] = remote(
                pkt3.at[d, j, pl.ds(S, S // 2)], pkt4.at[j, pl.ds(d * (S // 2), S // 2)],
                h_s.at[3, j, d], h_r.at[3, j, d], zpeer(dz),
            )
        for d in range(2):
            xsend(j, lambda n: pkt3.at[d, j, pl.ds(n, 1)], 1, 5 + d)

    def xb(j):
        for d in range(2):
            hops[4, j, d].wait_recv()
        xsend(j, lambda n: pkt4.at[j, pl.ds(n, 1)], 1, 7)

    def cross(j):
        @pl.loop(0, 2 * G)
        def _(n):
            csel[j, n] = hists[0][j][pl.ds(slag[0, 1, n], STEPS)]

        dst = recvs[j].at[pl.ds(Z * S + 2 * g, 2)]
        for i in range(1, G):
            h = lax.rem(g + i, G)
            remote(csel.at[j, pl.ds(2 * h, 2)], dst, x_s.at[j], x_r.at[j], (h, dev))
        pltpu.make_async_copy(csel.at[j, pl.ds(2 * g, 2)], dst, x_r.at[j]).start()

    def compute(j):
        pltpu.make_async_copy(recvs[j], recvs[j], x_r.at[j]).wait()
        cum[TILES] = jnp.zeros((ROWS, W), F32)

        def body(i, acc):
            v = recvs[j][ssrt[1, i]].reshape(ROWS, W)
            t = tiles[ssrt[0, i]]
            acc = acc * ssrt[2, i].astype(F32) + jnp.dot(v, t, preferred_element_type=F32)
            cum[i] = acc
            return acc

        lax.fori_loop(0, TILES, body, jnp.zeros((ROWS, W), F32), unroll=UNROLL)

    rs = {}

    def rs1(j):
        b = j % 2
        if j >= 2:
            rs[1, j - 2].wait_send()

        @pl.loop(0, X * Z)
        def _(n):
            e = (lax.rem(n, Z) * X + n // Z) * C + 1 - c
            send1[b, n] = cum[ssrt[3, e]].astype(SEND1)

        rs[1, j] = remote(send1.at[b], r1.at[j], rs_s.at[0, j, 0], rs_r.at[0, j, 0], at(z, x, 1 - c))

    def rs2(j):
        b = j % 2
        rs[1, j].wait_recv()
        if j >= 2:
            for i in range(1, X):
                rs[2, j - 2, i].wait_send()
        for i in range(1, X):
            xx = lax.rem(x + i, X)

            @pl.loop(0, Z)
            def _(n):
                total = cum[ssrt[3, (n * X + xx) * C + c]] + r1[j, xx * Z + n].astype(F32)
                send2[b, i - 1, n] = total.astype(SEND2)

            rs[2, j, i] = remote(
                send2.at[b, i - 1], r2.at[j, i - 1], rs_s.at[1, j, i], rs_r.at[1, j, i], at(z, xx, c)
            )

        @pl.loop(0, Z)
        def _(n):
            own2[b, n] = cum[ssrt[3, (n * X + x) * C + c]] + r1[j, x * Z + n].astype(F32)

    def rs3(j):
        b = j % 2
        for i in range(1, X):
            rs[2, j, i].wait_recv()
        if j >= 2:
            for i in range(1, Z):
                rs[3, j - 2, i].wait_send()
        for i in range(Z):
            n = lax.rem(z + i, Z)
            total = own2[b, n] + r2[j, 0, n].astype(F32) + r2[j, 1, n].astype(F32) + r2[j, 2, n].astype(F32)
            if i == 0:
                own3[b] = total
            else:
                send3[b, i - 1] = total.astype(SEND3)
                rs[3, j, i] = remote(
                    send3.at[b, i - 1], r3.at[j, i - 1], rs_s.at[2, j, i], rs_r.at[2, j, i], zpeer(i)
                )

    def rs4(j):
        b = j % 2
        total = own3[b]
        for i in range(1, Z):
            rs[3, j, i].wait_recv()
            total = total + r3[j, i - 1].astype(F32)
        rows = pl.ds(j * RC, RC)
        one, two = hists[0][j][0], hists[0][j][1]
        inverse = jac[...]
        for k in range(STEPS):
            part = total[(STEPS - 1 - k) * RC : (STEPS - k) * RC]
            term = jnp.dot(one, selft[0], preferred_element_type=F32)
            term = term + jnp.dot(two, selft[1], preferred_element_type=F32)
            resid = inc[k, rows] - part - term
            value = jnp.dot(resid, inverse, precision=lax.Precision.HIGHEST, preferred_element_type=F32)
            out[k, rows] = value
            two, one = one, value.astype(BF16)

    def order():
        lane = lax.broadcasted_iota(I32, (128, 128), 1)
        sub = lax.broadcasted_iota(I32, (128, 128), 0)
        by_lane = jnp.where(lane < TILES, jnp.broadcast_to(meta[3:4, :], (128, 128)), 127)
        by_sub = by_lane.T
        q = meta[2:3, :]
        dz = lax.rem(z - q // S + Z, Z)
        o = jnp.where(dz == 1, 1, 0)
        for d, place in ((7, 2), (2, 3), (6, 4), (3, 5), (5, 6), (4, 7)):
            o = jnp.where(dz == d, place, o)
        place = jnp.where(q < Z * S, lax.rem(q, S) * Z + o, q)
        place = jnp.broadcast_to(place, (128, 128)).T
        same = jnp.where((by_lane == by_sub) & (lane < sub), 1, 0)
        before = jnp.where(by_lane < by_sub, 1, 0) + same
        rank = jnp.sum(before, axis=1, keepdims=True)
        goes_on = jnp.where(jnp.sum(same, axis=1, keepdims=True) > 0, 1, 0)
        hot = jnp.where(rank == lane, 1, 0)
        upto = jnp.sum(jnp.where(by_sub <= lane, 1, 0), axis=0, keepdims=True)
        count = jnp.sum(jnp.where(by_sub == lane, 1, 0), axis=0, keepdims=True)
        srt[0:1, :] = jnp.sum(hot * sub, axis=0, keepdims=True)
        srt[1:2, :] = jnp.sum(hot * place, axis=0, keepdims=True)
        srt[2:3, :] = jnp.sum(hot * goes_on, axis=0, keepdims=True)
        srt[3:4, :] = jnp.where(count > 0, upto - 1, TILES)
        srt[4:8, :] = jnp.zeros((4, 128), I32)

    lags = []
    for i, dz in enumerate((1, -1, 2, -2)):
        lags.append(remote(meta, lagbuf.at[1 + i], lag_s.at[i], lag_r.at[i], zpeer(dz)))
    h1(0)
    h1(1)
    for cp in big:
        cp.start()
    lagbuf[0] = meta[...]
    order()
    for cp in lags:
        cp.wait_recv()
    cp = pltpu.make_async_copy(lagbuf, slag, small_sem.at[0])
    cp.start()
    cp2 = pltpu.make_async_copy(srt, ssrt, small_sem.at[1])
    cp2.start()
    cp.wait()
    cp2.wait()
    cross(0)
    cross(1)

    h2(0)
    h2(1)
    h3(0)
    h1(2)
    xa(0)
    h4(0)
    h3(1)
    xa(1)
    cross(2)
    h2(2)
    xb(0)
    h4(1)
    h1(3)
    h3(2)
    for cp in big:
        cp.wait()
    compute(0)
    rs1(0)
    xa(2)
    cross(3)
    h2(3)
    rs2(0)
    xb(1)
    h4(2)
    compute(1)
    rs1(1)
    rs3(0)
    h3(3)
    xa(3)
    rs2(1)
    xb(2)
    rs4(0)
    rs3(1)
    h4(3)
    compute(2)
    rs1(2)
    xb(3)
    rs2(2)
    rs4(1)
    compute(3)
    rs1(3)
    rs3(2)
    rs2(3)
    rs4(2)
    rs3(3)
    rs4(3)

    for cp in lags:
        cp.wait_send()
    for cp in hops.values():
        cp.wait_send()
    for j in range(CH):
        away = (S - 1) * Z + 2 * (G - 1)
        pltpu.make_async_copy(recvs[j].at[pl.ds(0, away)], recvs[j].at[pl.ds(0, away)], x_s.at[j]).wait()
    for j in range(CH - 2, CH):
        rs[1, j].wait_send()
        for i in range(1, X):
            rs[2, j, i].wait_send()
        for i in range(1, Z):
            rs[3, j, i].wait_send()


def per_device(
    history, incident, jacobi, self_tiles, near_tiles, send_lag, cross_lag, tile_slot, tile_dest
):
    def row(a):
        flat = a.reshape(1, -1)
        return jnp.pad(flat, ((0, 0), (0, 128 - flat.shape[1])))

    meta = jnp.concatenate(
        [row(send_lag - STEPS), row(cross_lag - STEPS), row(tile_slot), row(tile_dest), jnp.zeros((4, 128), I32)]
    )
    dma = pltpu.SemaphoreType.DMA
    hbm = pl.BlockSpec(memory_space=pl.ANY)
    vmem = pl.BlockSpec(memory_space=pltpu.VMEM)
    piece = (STEPS, RC, W)
    out = pl.pallas_call(
        kernel,
        out_shape=jax.ShapeDtypeStruct((STEPS, R, W), F32),
        in_specs=[vmem, hbm, hbm, hbm, hbm, hbm],
        out_specs=vmem,
        scratch_shapes=[
            [[pltpu.VMEM((LAGS, RC, W), BF16)] * CH] * 5,
            pltpu.VMEM((2, CH, S + S // 2, *piece), BF16),
            pltpu.VMEM((CH, S, *piece), BF16),
            pltpu.VMEM((2, CH, S + S // 2, *piece), BF16),
            pltpu.VMEM((CH, S, 5, *piece), BF16),
            pltpu.VMEM((CH, 2 * G, *piece), BF16),
            [pltpu.VMEM((SLOTS, *piece), BF16)] * CH,
            pltpu.VMEM((TILES, W, W), BF16),
            pltpu.VMEM((STEPS, R, W), F32),
            pltpu.VMEM((W, W), F32),
            pltpu.VMEM((2, W, W), BF16),
            pltpu.VMEM((TILES + 1, ROWS, W), F32),
            pltpu.VMEM((2, X * Z, ROWS, W), SEND1),
            pltpu.VMEM((CH, X * Z, ROWS, W), SEND1),
            pltpu.VMEM((2, X - 1, Z, ROWS, W), SEND2),
            pltpu.VMEM((2, Z, ROWS, W), F32),
            pltpu.VMEM((CH, X - 1, Z, ROWS, W), SEND2),
            pltpu.VMEM((2, Z - 1, ROWS, W), SEND3),
            pltpu.VMEM((2, ROWS, W), F32),
            pltpu.VMEM((CH, Z - 1, ROWS, W), SEND3),
            pltpu.VMEM((5, 8, 128), I32),
            pltpu.VMEM((8, 128), I32),
            pltpu.SMEM((5, 8, 128), I32),
            pltpu.SMEM((8, 128), I32),
            dma((CH,)),
            dma((4,)),
            dma((4,)),
            dma((4,)),
            dma((2,)),
            dma((4, CH, 2)),
            dma((4, CH, 2)),
            dma((CH,)),
            dma((CH,)),
            dma((3, CH, Z)),
            dma((3, CH, Z)),
        ],
        compiler_params=pltpu.CompilerParams(
            collective_id=0, has_side_effects=True, vmem_limit_bytes=62 * 2**20
        ),
    )(meta, history[0], incident[0], jacobi[0], self_tiles[0], near_tiles[0])
    return out[None]


def solution(mesh):
    spec = P(("group", "dev"))
    return jax.shard_map(
        per_device, mesh=mesh, in_specs=(spec,) * 9, out_specs=spec, check_vma=False
    )
```

time: 492 us -> 183 us (0.37)
  waiting for transfers between devices: 321 us -> 0 us
  Pallas kernels: 0 us -> 177 us
  local copies, waits for them, and re-layouts: 51.3 us -> 3.74 us
  other arithmetic: 42 us -> 1.34 us
  starting transfers between devices: 38.5 us -> 0 us
  matrix products: 20.9 us -> 0 us
  between operations: 13.9 us -> 0.01 us
    unnamed x2 -> x0, waiting for transfers between devices: 215 us -> none
    pallas_call x0 -> x1, Pallas kernels: none -> 177 us  [per_device(): pl.pallas_call(kernel, out_shape=jax.ShapeDtypeStruct((STEPS, R, W), F32)...]
    all_to_all x6 -> x0, waiting for transfers between devices: 106 us -> none  [the longest x3 98.3 us: per_device(): lax.all_to_all(blocks, 'dev', split_axis=0, concat_axis=0, tiled=True)]
    all_to_all x6 -> x0, starting transfers between devices: 38 us -> none  [the longest x3 22.7 us: per_device(): lax.all_to_all(blocks, 'dev', split_axis=0, concat_axis=0, tiled=True)]
    scatter-add x3 -> x0, other arithmetic: 30.7 us -> none  [prepare_terms(): grouped = jax.ops.segment_sum(flat, tile_dest[0], num_segments=ndev)]
    gather x9 -> x0, local copies, waits for them, and re-layouts: 26.2 us -> none  [the longest x3 12.1 us: prepare_terms(): values = received[:, tile_slot[0]]]
    unnamed x23 -> x1, local copies, waits for them, and re-layouts: 24.5 us -> 1.62 us
    dot_general x12 -> x0, matrix products: 20.9 us -> none  [the longest x3 19.3 us: prepare_terms(): jnp.einsum('strp,tpq->tsrq', values, tiles, preferred_element_type=jnp.fl...]
  transfers between devices with their start and end apart: 7 -> 0, of which waited for: 6 -> 0; matrix products, arithmetic and copies ran while one was open for 15% -> 0% of each run, Pallas kernels for 0% -> 0%
where the time goes in v1:
time: 183 us; the launch traced here: 182 us
  Pallas kernels  177 us (97%)
  local copies, waits for them, and re-layouts  3.74 us (2%)
    pallas_call x1, Pallas kernels, per_device(): pl.pallas_call(kernel, out_shape=jax.ShapeDtypeStruct((STEPS, R, W), F32)...  177 us

profile of v1, /device:TPU:8, one launch (start us, length us, event | category | flops | bytes accessed | tf_op | source)
XLA Modules:
  0.0 182.2 jit_solution(3923680722000263378)
XLA Ops:
  0.0 0.7 add_bitcast_fusion
  0.7 0.7 pad.17
  1.3 0.7 pad.18
  2.0 0.7 broadcast_add_fusion
  2.7 0.1 copy.11
  2.8 0.1 reshape.7
  2.9 0.6 concatenate.3.meta
  3.5 177.1 %shard_map.91 = f32[3,64,256]{2,1,0:T(8,128)} custom-call(s32[8,128]{1,0:T(8,128)} %concatenate.3.meta, bf16[48,64,256]{2,1,0:T(8,128)(2,1)} %bitcast.9, f32[3,64,256]{2,1,0:T(8,128)} %bitcast.13, f32[256,256]{1,0:T(8,128)} %bitcast.11, bf16[2,256,256]{2,1,0:T(8,128)(2,1)} %bitcast.12, bf16[76,256,256]{2,1,0:T(8,128)(2,1)} %bitcast.8), custom_call_target="tpu_custom_call" | custom-call | tf_op jit(solution)/shard_map/pallas_call | solution.py:350
  180.6 1.6 copy.13
  (3 shorter events, 0.0 us)

commit v2 on v1

--- a/solution.py
+++ b/solution.py
@@ -18,15 +18,17 @@
 RC = R // CH
 ROWS = STEPS * RC
 F32, BF16, I32 = jnp.float32, jnp.bfloat16, jnp.int32
-SEND1, SEND2, SEND3 = F32, BF16, BF16
+SEND1, SEND2, SEND3 = F32, BF16, F32
 UNROLL = 4
+PIECES = 4
+ZP = Z // PIECES
 
 
 def kernel(
-    meta, hist, inc_hbm, jac_hbm, self_hbm, tiles_hbm, out,
+    send_lag, cross_lag, tile_slot, tile_dest, hist, inc_hbm, jac_hbm, self_hbm, tiles_hbm, out,
     hists, pkt3, pkt4, fsel, sel, csel, recvs, tiles, inc, jac, selft,
     cum, send1, r1, send2, own2, r2, send3, own3, r3,
-    lagbuf, srt, slag, ssrt,
+    meta, lagbuf, srt, slag, ssrt,
     load_sem, in_sem, lag_s, lag_r, small_sem,
     h_s, h_r, x_s, x_r, rs_s, rs_r,
 ):
@@ -62,6 +64,12 @@
         pltpu.make_async_copy(self_hbm, selft, in_sem.at[3]),
     ]
 
+    meta[...] = jnp.zeros((8, 128), I32)
+    meta[0:1, 0 : Z * S] = jnp.maximum(send_lag[...] - STEPS, 0)
+    meta[2:3, 0:TILES] = tile_slot[...]
+    meta[3:4, 0:TILES] = tile_dest[...]
+    meta[4 : 4 + G, 0:2] = jnp.maximum(cross_lag[...] - STEPS, 0)
+
     barrier = pltpu.get_barrier_semaphore()
     for dz in range(1, Z):
         pl.semaphore_signal(barrier, inc=1, device_id=zpeer(dz), device_id_type=MESH)
@@ -75,7 +83,6 @@
     hops = {}
 
     def h1(j):
-        loads[j].wait()
         for d, dz in ((0, 1), (1, -1)):
             hops[1, j, d] = remote(hists[0][j], hists[1 + d][j], h_s.at[0, j, d], h_r.at[0, j, d], zpeer(dz))
 
@@ -106,14 +113,14 @@
             remote(pick(n), recvs[j].at[pl.ds(me * Z + col, width)], x_s.at[j], x_r.at[j], plane(n))
         pltpu.make_async_copy(pick(me), recvs[j].at[pl.ds(me * Z + col, width)], x_r.at[j]).start()
 
-    def xa(j):
-        for o in range(5):
+    def xa(j, lo, hi):
+        for o in range(lo, hi):
 
             @pl.loop(0, S)
             def _(n):
                 sel[j, n, o] = hists[o][j][pl.ds(slag[o, 0, z * S + n], STEPS)]
 
-        xsend(j, lambda n: sel.at[j, n], 5, 0)
+        xsend(j, lambda n: sel.at[j, n, pl.ds(lo, hi - lo)], hi - lo, lo)
 
     def h4(j):
         for d, dz in ((0, 1), (1, -1)):
@@ -133,7 +140,7 @@
     def cross(j):
         @pl.loop(0, 2 * G)
         def _(n):
-            csel[j, n] = hists[0][j][pl.ds(slag[0, 1, n], STEPS)]
+            csel[j, n] = hists[0][j][pl.ds(slag[0, 4 + n // 2, lax.rem(n, 2)], STEPS)]
 
         dst = recvs[j].at[pl.ds(Z * S + 2 * g, 2)]
         for i in range(1, G):
@@ -159,72 +166,81 @@
     def rs1(j):
         b = j % 2
         if j >= 2:
-            rs[1, j - 2].wait_send()
-
-        @pl.loop(0, X * Z)
-        def _(n):
-            e = (lax.rem(n, Z) * X + n // Z) * C + 1 - c
-            send1[b, n] = cum[ssrt[3, e]].astype(SEND1)
-
-        rs[1, j] = remote(send1.at[b], r1.at[j], rs_s.at[0, j, 0], rs_r.at[0, j, 0], at(z, x, 1 - c))
-
-    def rs2(j):
+            for p in range(PIECES):
+                rs[1, j - 2, p].wait_send()
+        for p in range(PIECES):
+
+            @pl.loop(0, X * ZP)
+            def _(n):
+                e = (lax.rem(z + 1 + p * ZP + lax.rem(n, ZP), Z) * X + n // ZP) * C + 1 - c
+                send1[b, p, n] = cum[ssrt[3, e]].astype(SEND1)
+
+            rs[1, j, p] = remote(
+                send1.at[b, p], r1.at[j, p], rs_s.at[0, j, p], rs_r.at[0, j, p], at(z, x, 1 - c)
+            )
+
+    def rs2(j, p):
         b = j % 2
-        rs[1, j].wait_recv()
+        rs[1, j, p].wait_recv()
         if j >= 2:
             for i in range(1, X):
-                rs[2, j - 2, i].wait_send()
+                rs[2, j - 2, p, i].wait_send()
+
+        def total(xx, n):
+            zz = lax.rem(z + 1 + p * ZP + n, Z)
+            return cum[ssrt[3, (zz * X + xx) * C + c]] + r1[j, p, xx * ZP + n].astype(F32)
+
         for i in range(1, X):
             xx = lax.rem(x + i, X)
-
-            @pl.loop(0, Z)
-            def _(n):
-                total = cum[ssrt[3, (n * X + xx) * C + c]] + r1[j, xx * Z + n].astype(F32)
-                send2[b, i - 1, n] = total.astype(SEND2)
-
-            rs[2, j, i] = remote(
-                send2.at[b, i - 1], r2.at[j, i - 1], rs_s.at[1, j, i], rs_r.at[1, j, i], at(z, xx, c)
+            for n in range(ZP):
+                send2[b, p, i - 1, n] = total(xx, n).astype(SEND2)
+            q = p * X + i
+            rs[2, j, p, i] = remote(
+                send2.at[b, p, i - 1], r2.at[j, p, i - 1], rs_s.at[1, j, q], rs_r.at[1, j, q], at(z, xx, c)
             )
-
-        @pl.loop(0, Z)
-        def _(n):
-            own2[b, n] = cum[ssrt[3, (n * X + x) * C + c]] + r1[j, x * Z + n].astype(F32)
-
-    def rs3(j):
+        for n in range(ZP):
+            own2[b, p, n] = total(x, n)
+
+    def rs3(j, p):
         b = j % 2
         for i in range(1, X):
-            rs[2, j, i].wait_recv()
-        if j >= 2:
-            for i in range(1, Z):
-                rs[3, j - 2, i].wait_send()
-        for i in range(Z):
-            n = lax.rem(z + i, Z)
-            total = own2[b, n] + r2[j, 0, n].astype(F32) + r2[j, 1, n].astype(F32) + r2[j, 2, n].astype(F32)
-            if i == 0:
-                own3[b] = total
+            rs[2, j, p, i].wait_recv()
+        for n in range(ZP):
+            i = p * ZP + n
+            total = own2[b, p, n]
+            for k in range(X - 1):
+                total = total + r2[j, p, k, n].astype(F32)
+            if i == Z - 1:
+                own3[j] = total
             else:
-                send3[b, i - 1] = total.astype(SEND3)
-                rs[3, j, i] = remote(
-                    send3.at[b, i - 1], r3.at[j, i - 1], rs_s.at[2, j, i], rs_r.at[2, j, i], zpeer(i)
-                )
+                if j >= 2:
+                    rs[3, j - 2, i].wait_send()
+                send3[b, i] = total.astype(SEND3)
+                rs[3, j, i] = remote(send3.at[b, i], r3.at[j, i], rs_s.at[2, j, i], rs_r.at[2, j, i], zpeer(i + 1))
 
     def rs4(j):
-        b = j % 2
-        total = own3[b]
-        for i in range(1, Z):
+        rows = pl.ds(j * RC, RC)
+        first, second = selft[0], selft[1]
+        one, two = hists[0][j][0], hists[0][j][1]
+
+        def dot(u, v):
+            return jnp.dot(u, v, preferred_element_type=F32)
+
+        known = [dot(one, first) + dot(two, second), dot(one, second)]
+        total = own3[j]
+        for i in range(Z - 1):
             rs[3, j, i].wait_recv()
-            total = total + r3[j, i - 1].astype(F32)
-        rows = pl.ds(j * RC, RC)
-        one, two = hists[0][j][0], hists[0][j][1]
+            total = total + r3[j, i].astype(F32)
         inverse = jac[...]
+        past = []
         for k in range(STEPS):
-            part = total[(STEPS - 1 - k) * RC : (STEPS - k) * RC]
-            term = jnp.dot(one, selft[0], preferred_element_type=F32)
-            term = term + jnp.dot(two, selft[1], preferred_element_type=F32)
-            resid = inc[k, rows] - part - term
+            term = known[k] if k < 2 else dot(past[k - 2], second)
+            if k > 0:
+                term = term + dot(past[k - 1], first)
+            resid = inc[k, rows] - total[(STEPS - 1 - k) * RC : (STEPS - k) * RC] - term
             value = jnp.dot(resid, inverse, precision=lax.Precision.HIGHEST, preferred_element_type=F32)
             out[k, rows] = value
-            two, one = one, value.astype(BF16)
+            past.append(value.astype(BF16))
 
     def order():
         lane = lax.broadcasted_iota(I32, (128, 128), 1)
@@ -251,6 +267,8 @@
         srt[3:4, :] = jnp.where(count > 0, upto - 1, TILES)
         srt[4:8, :] = jnp.zeros((4, 128), I32)
 
+    for cp in loads:
+        cp.wait()
     lags = []
     for i, dz in enumerate((1, -1, 2, -2)):
         lags.append(remote(meta, lagbuf.at[1 + i], lag_s.at[i], lag_r.at[i], zpeer(dz)))
@@ -271,53 +289,72 @@
     cross(0)
     cross(1)
 
+    xa(0, 0, 1)
+    xa(1, 0, 1)
     h2(0)
+    xa(0, 1, 3)
     h2(1)
+    xa(1, 1, 3)
     h3(0)
     h1(2)
-    xa(0)
+    xa(0, 3, 5)
+    xa(2, 0, 1)
+    xa(3, 0, 1)
     h4(0)
     h3(1)
-    xa(1)
+    xa(1, 3, 5)
     cross(2)
+    cross(3)
     h2(2)
+    xa(2, 1, 3)
     xb(0)
     h4(1)
     h1(3)
     h3(2)
+    xa(2, 3, 5)
     for cp in big:
         cp.wait()
     compute(0)
     rs1(0)
-    xa(2)
-    cross(3)
     h2(3)
-    rs2(0)
+    xa(3, 1, 3)
+    for p in range(PIECES):
+        rs2(0, p)
     xb(1)
     h4(2)
     compute(1)
     rs1(1)
-    rs3(0)
+    for p in range(PIECES):
+        rs3(0, p)
     h3(3)
-    xa(3)
-    rs2(1)
+    xa(3, 3, 5)
+    for p in range(PIECES):
+        rs2(1, p)
     xb(2)
     rs4(0)
-    rs3(1)
+    for p in range(PIECES):
+        rs3(1, p)
     h4(3)
     compute(2)
     rs1(2)
     xb(3)
-    rs2(2)
+    for p in range(PIECES):
+        rs2(2, p)
     rs4(1)
     compute(3)
     rs1(3)
-    rs3(2)
-    rs2(3)
+    for p in range(PIECES):
+        rs3(2, p)
+    rs2(3, 0)
+    rs2(3, 1)
+    rs3(3, 0)
+    rs2(3, 2)
+    rs3(3, 1)
+    rs2(3, 3)
+    rs3(3, 2)
+    rs3(3, 3)
     rs4(2)
-    rs3(3)
     rs4(3)
-
     for cp in lags:
         cp.wait_send()
     for cp in hops.values():
@@ -326,23 +363,17 @@
         away = (S - 1) * Z + 2 * (G - 1)
         pltpu.make_async_copy(recvs[j].at[pl.ds(0, away)], recvs[j].at[pl.ds(0, away)], x_s.at[j]).wait()
     for j in range(CH - 2, CH):
-        rs[1, j].wait_send()
-        for i in range(1, X):
-            rs[2, j, i].wait_send()
-        for i in range(1, Z):
+        for p in range(PIECES):
+            rs[1, j, p].wait_send()
+            for i in range(1, X):
+                rs[2, j, p, i].wait_send()
+        for i in range(Z - 1):
             rs[3, j, i].wait_send()
 
 
 def per_device(
     history, incident, jacobi, self_tiles, near_tiles, send_lag, cross_lag, tile_slot, tile_dest
 ):
-    def row(a):
-        flat = a.reshape(1, -1)
-        return jnp.pad(flat, ((0, 0), (0, 128 - flat.shape[1])))
-
-    meta = jnp.concatenate(
-        [row(send_lag - STEPS), row(cross_lag - STEPS), row(tile_slot), row(tile_dest), jnp.zeros((4, 128), I32)]
-    )
     dma = pltpu.SemaphoreType.DMA
     hbm = pl.BlockSpec(memory_space=pl.ANY)
     vmem = pl.BlockSpec(memory_space=pltpu.VMEM)
@@ -350,7 +381,7 @@
     out = pl.pallas_call(
         kernel,
         out_shape=jax.ShapeDtypeStruct((STEPS, R, W), F32),
-        in_specs=[vmem, hbm, hbm, hbm, hbm, hbm],
+        in_specs=[vmem] * 4 + [hbm] * 5,
         out_specs=vmem,
         scratch_shapes=[
             [[pltpu.VMEM((LAGS, RC, W), BF16)] * CH] * 5,
@@ -365,14 +396,15 @@
             pltpu.VMEM((W, W), F32),
             pltpu.VMEM((2, W, W), BF16),
             pltpu.VMEM((TILES + 1, ROWS, W), F32),
-            pltpu.VMEM((2, X * Z, ROWS, W), SEND1),
-            pltpu.VMEM((CH, X * Z, ROWS, W), SEND1),
-            pltpu.VMEM((2, X - 1, Z, ROWS, W), SEND2),
-            pltpu.VMEM((2, Z, ROWS, W), F32),
-            pltpu.VMEM((CH, X - 1, Z, ROWS, W), SEND2),
+            pltpu.VMEM((2, PIECES, X * ZP, ROWS, W), SEND1),
+            pltpu.VMEM((CH, PIECES, X * ZP, ROWS, W), SEND1),
+            pltpu.VMEM((2, PIECES, X - 1, ZP, ROWS, W), SEND2),
+            pltpu.VMEM((2, PIECES, ZP, ROWS, W), F32),
+            pltpu.VMEM((CH, PIECES, X - 1, ZP, ROWS, W), SEND2),
             pltpu.VMEM((2, Z - 1, ROWS, W), SEND3),
-            pltpu.VMEM((2, ROWS, W), F32),
+            pltpu.VMEM((CH, ROWS, W), F32),
             pltpu.VMEM((CH, Z - 1, ROWS, W), SEND3),
+            pltpu.VMEM((8, 128), I32),
             pltpu.VMEM((5, 8, 128), I32),
             pltpu.VMEM((8, 128), I32),
             pltpu.SMEM((5, 8, 128), I32),
@@ -386,13 +418,15 @@
             dma((4, CH, 2)),
             dma((CH,)),
             dma((CH,)),
-            dma((3, CH, Z)),
-            dma((3, CH, Z)),
+            dma((3, CH, PIECES * X)),
+            dma((3, CH, PIECES * X)),
         ],
         compiler_params=pltpu.CompilerParams(
             collective_id=0, has_side_effects=True, vmem_limit_bytes=62 * 2**20
         ),
-    )(meta, history[0], incident[0], jacobi[0], self_tiles[0], near_tiles[0])
+    )(
+        send_lag.reshape(1, -1), cross_lag[0], tile_slot, tile_dest, history[0], incident[0], jacobi[0], self_tiles[0], near_tiles[0]
+    )
     return out[None]
 
 

time: 183 us -> 176 us (0.962)
  Pallas kernels: 177 us -> 173 us
    pallas_call x1, Pallas kernels: 177 us -> 173 us  [per_device(): pl.pallas_call(kernel, out_shape=jax.ShapeDtypeStruct((STEPS, R, W), F32)...]
where the time goes in v2:
time: 176 us
  Pallas kernels  173 us (98%)
  local copies, waits for them, and re-layouts  2.95 us (2%)
    pallas_call x1, Pallas kernels, per_device(): pl.pallas_call(kernel, out_shape=jax.ShapeDtypeStruct((STEPS, R, W), F32)...  173 us

profile of v2, /device:TPU:8, one launch (start us, length us, event | category | flops | bytes accessed | tf_op | source)
XLA Modules:
  0.0 176.3 jit_solution(16218738484056344749)
XLA Ops:
  0.0 1.3 copy.10.cross_lag
  1.3 173.4 %shard_map.91 = f32[3,64,256]{2,1,0:T(8,128)} custom-call(s32[1,64]{1,0:T(1,128)} %bitcast.15, s32[4,2]{1,0:T(4,128)} %copy.10.cross_lag, s32[1,76]{1,0:T(1,128)} %tile_slot.1, s32[1,76]{1,0:T(1,128)} %tile_dest.1, bf16[48,64,256]{2,1,0:T(8,128)(2,1)} %bitcast.9, f32[3,64,256]{2,1,0:T(8,128)} %bitcast.13, f32[256,256]{1,0:T(8,128)} %bitcast.11, ...), custom_call_target="tpu_custom_call" | custom-call | tf_op jit(solution)/shard_map/pallas_call | solution.py:381
  174.7 1.6 copy.12
